TPU v7x, 32 devices: a whole 2x2x4 slice. The times are simulated.
32 devices in a mesh: ctx: 16 (over z, x, core), tp: 2 (over y).
Axes of the slice: x: 2, y: 2, z: 4, core: 2. Of those that a mesh axis runs over, the one named last changes fastest.
Arguments:
- queries: bfloat16 [2048, 4096], P('ctx', 'tp'), may hold values from -5 to 5
- keys: bfloat16 [2048, 1024], P('ctx', 'tp'), may hold values from -5 to 5
- values: bfloat16 [2048, 1024], P('ctx', 'tp'), may hold values from -6 to 6
- docs: int32 [2048], P('ctx'), may hold values from 0 to 11, never falling along the last dimension, each value on 1 to 1152 neighbouring positions
- out_weight: bfloat16 [4096, 4096], P('tp'), may hold values from -0.09375 to 0.09375
Outputs:
- mixed: bfloat16 [2048, 4096], P('ctx', 'tp')
All inputs are finite; a program needn't handle non-finite values.
Results may differ from a plain program's by a relative error of at most 0.014.
Values may be sent and summed in bfloat16 or wider, within the bound.
A program may use at most 64 MiB of HBM per device.

v0:
```python
import math

import jax
import jax.numpy as jnp
from jax import lax
from jax.sharding import PartitionSpec as P

HEAD_DIM = 128


neg_large = -1e30


def attend(state, query_half, query_pos, query_doc, key_part, value_part, key_pos, key_doc):
    peak, total, accum = state
    scores = jnp.einsum("igkd,jgd->gkij", query_half, key_part, preferred_element_type=jnp.float32)
    scores = scores * (1.0 / math.sqrt(key_part.shape[-1]))
    allowed = (key_pos[None, :] <= query_pos[:, None]) & (key_doc[None, :] == query_doc[:, None])
    block_peak = jnp.max(jnp.where(allowed, scores, neg_large), axis=-1)
    new_peak = jnp.maximum(peak, block_peak)
    rescale = jnp.exp(peak - new_peak)
    weights = jnp.where(allowed, jnp.exp(scores - new_peak[..., None]), 0.0)
    total = total * rescale + jnp.sum(weights, axis=-1)
    update = jnp.einsum(
        "gkij,jgd->gkid",
        weights.astype(jnp.bfloat16),
        value_part,
        preferred_element_type=jnp.float32,
    )
    accum = accum * rescale[..., None] + update
    return (new_peak, total, accum)


def visit(state, query_half, query_pos, query_doc, key_part, value_part, key_pos, key_doc):
    needed = jnp.min(key_pos) <= jnp.max(query_pos)

    def compute(current):
        return attend(
            current, query_half, query_pos, query_doc, key_part, value_part, key_pos, key_doc
        )

    def unchanged(current):
        return current

    return lax.cond(needed, compute, unchanged, state)


def finish(state):
    peak, total, accum = state
    summed = accum / total[..., None]
    kv_count, group_size, row_count, head_dim = summed.shape
    summed = jnp.transpose(summed, (2, 0, 1, 3)).reshape(
        row_count, kv_count * group_size * head_dim
    )
    return summed.astype(jnp.bfloat16)


def shards(queries, keys, values, docs, out_weight):
    row_count = queries.shape[0]
    half_rows = row_count // 2
    head_dim = HEAD_DIM
    kv_local = keys.shape[1] // head_dim
    group_size = queries.shape[1] // keys.shape[1]
    my_index = lax.axis_index("ctx")
    all_docs = lax.all_gather(docs, "ctx", axis=0, tiled=True)
    offsets = jnp.arange(half_rows, dtype=jnp.int32)
    shard_offsets = jnp.arange(row_count, dtype=jnp.int32)
    lower_queries = queries[:half_rows]
    upper_queries = queries[half_rows:]
    low_positions = my_index * row_count + offsets
    high_positions = my_index * row_count + half_rows + offsets
    low_docs = jnp.take(all_docs, low_positions)
    high_docs = jnp.take(all_docs, high_positions)
    query_low = lower_queries.reshape(half_rows, kv_local, group_size, head_dim)
    query_high = upper_queries.reshape(half_rows, kv_local, group_size, head_dim)
    empty = (
        jnp.full((kv_local, group_size, half_rows), neg_large, jnp.float32),
        jnp.zeros((kv_local, group_size, half_rows), jnp.float32),
        jnp.zeros((kv_local, group_size, half_rows, head_dim), jnp.float32),
    )
    carry = (empty, empty)
    key_piece = lax.all_gather(keys, "ctx", axis=0, tiled=True)
    value_piece = lax.all_gather(values, "ctx", axis=0, tiled=True)
    shard_count = key_piece.shape[0] // row_count
    shaped_keys = key_piece.reshape(shard_count, row_count, kv_local, head_dim)
    shaped_values = value_piece.reshape(shard_count, row_count, kv_local, head_dim)
    shard_numbers = jnp.arange(shard_count, dtype=jnp.int32)

    def one_shard(states, inputs):
        key_part, value_part, shard_number = inputs
        key_pos = shard_number * row_count + shard_offsets
        key_doc = jnp.take(all_docs, key_pos)
        state_low, state_high = states
        state_low = visit(
            state_low, query_low, low_positions, low_docs, key_part, value_part, key_pos, key_doc
        )
        state_high = visit(
            state_high,
            query_high,
            high_positions,
            high_docs,
            key_part,
            value_part,
            key_pos,
            key_doc,
        )
        return ((state_low, state_high), None)

    carry, unused = lax.scan(one_shard, carry, (shaped_keys, shaped_values, shard_numbers))
    attention = jnp.concatenate([finish(carry[0]), finish(carry[1])], axis=0)
    partial_terms = jnp.dot(attention, out_weight, preferred_element_type=jnp.float32)
    mixed = lax.psum_scatter(
        partial_terms.astype(jnp.bfloat16), "tp", scatter_dimension=1, tiled=True
    )
    return mixed


def solution(mesh):
    placed = (P("ctx", "tp"), P("ctx", "tp"), P("ctx", "tp"), P("ctx"), P("tp", None))
    return jax.shard_map(
        shards, mesh=mesh, in_specs=placed, out_specs=P("ctx", "tp"), check_vma=False
    )
```

profile of v0, /device:TPU:24, one launch (start us, length us, event | category | flops | bytes accessed | tf_op | source)
XLA Modules:
  0.0 294.0 jit_solution(883487180186446626)
XLA Ops:
  8.1 16.9 %all-gather = s32[16,1,128]{2,1,0:T(1,128)S(1)} all-gather(s32[1,1,128]{2,1,0:T(1,128)} %bitcast.89), channel_id=1, replica_groups=mesh['ctx'=16,'tp'=2] {'ctx'}, dimensions={0}, use_global_device_ids=true | all-gather | bytes 8704 | tf_op jit(solution)/shard_map/all_gather | solution.py:65
  28.8 21.9 %all-gather.4.cloned.1.call-done = bf16[2048,512]{1,0:T(8,128)(2,1)} async-done(((bf16[128,512]{1,0:T(8,128)(2,1)}), bf16[2048,512]{1,0:T(8,128)(2,1)}) %all-gather.4.cloned.1.call-update) | async-done | bytes 2097168 | tf_op jit(solution)/shard_map/all_gather | solution.py:82
  50.7 3.9 %reshape.104 = bf16[16,128,4,128]{3,2,1,0:T(4,128)(2,1)} reshape(bf16[2048,512]{1,0:T(8,128)(2,1)} %all-gather.4.cloned.1.call-done) | data formatting | bytes 4194304 | tf_op jit(solution)/shard_map/reshape | solution.py:85
  54.6 38.4 %all-gather.6.cloned.1.call-done = bf16[2048,512]{1,0:T(8,128)(2,1)} async-done(((bf16[128,512]{1,0:T(8,128)(2,1)}), bf16[2048,512]{1,0:T(8,128)(2,1)}) %all-gather.6.cloned.1.call-update) | async-done | bytes 2097168 | tf_op jit(solution)/shard_map/all_gather | solution.py:83
  93.1 4.0 %reshape.105 = bf16[16,128,4,128]{3,2,1,0:T(4,128)(2,1)} reshape(bf16[2048,512]{1,0:T(8,128)(2,1)} %all-gather.6.cloned.1.call-done) | data formatting | bytes 4194304 | tf_op jit(solution)/shard_map/reshape | solution.py:86
  97.2 150.3 %while.22 = (s32[]{:T(128)}, f32[4,4,64]{2,1,0:T(4,128)S(1)}, f32[4,4,64]{2,1,0:T(4,128)S(1)}, f32[4,4,64,128]{3,2,1,0:T(8,128)S(1)}, f32[4,4,64]{2,1,0:T(4,128)...) while((s32[]{:T(128)}, f32[4,4,64]{2,1,0:T(4,128)S(1)}, ...), condition=%wide.region_12.14_spmd.clone, body=%wide.region_2.13_spmd.clone.sunk | while | flops 137157504 | bytes 7549997 | solution.py:109
  102.7 1.5 conditional.7
  105.6 1.5 conditional.6
  112.6 1.5 conditional.7
  115.6 1.5 conditional.6
  122.6 1.5 conditional.7
  125.5 1.5 conditional.6
  132.6 1.5 conditional.7
  135.5 1.5 conditional.6
  152.5 1.5 conditional.7
  155.4 1.5 conditional.6
  172.4 1.5 conditional.7
  175.4 1.5 conditional.6
  192.4 1.5 conditional.7
  195.3 1.5 conditional.6
  212.3 1.5 conditional.7
  215.3 1.5 conditional.6
  248.7 9.1 %convolution_convert_fusion = bf16[128,4096]{1,0:T(8,128)(2,1)} fusion(bf16[2048,4096]{1,0:T(8,128)(2,1)} %param.17, bf16[64,2048]{1,0:T(8,128)(2,1)S(1)} %convert_element_type.40, bf16[64,2048]{1,0:T(8,128)(2,1)S(1)} %convert_element_type.37), kind=kOutput, calls=%fused_computation.51 | convolution fusion | flops 2149056512 | bytes 18350080 | tf_op jit(solution)/shard_map/dot_general | solution.py:111
  257.9 29.6 %reduce-scatter.2.cloned.1.call-done = bf16[128,2048]{1,0:T(8,128)(2,1)} async-done(((bf16[128,4096]{1,0:T(8,128)(2,1)}), bf16[128,2048]{1,0:T(8,128)(2,1)}) %reduce-scatter.2.cloned.1.call-update) | async-done | bytes 524304 | tf_op jit(solution)/shard_map/reduce_scatter | solution.py:112
  (432 shorter events, 117.8 us)
Async XLA Ops:
  6.5 44.2 %all-gather.4.cloned.1.call-start = ((), (), s32[]{:S(2)}) async-start(), calls=%async_computation.1 | async-start | bytes 2228224 | tf_op jit(solution)/shard_map/all_gather | solution.py:82
  7.3 85.8 %all-gather.6.cloned.1.call-start = ((), (), s32[]{:S(2)}) async-start(), calls=%async_computation.2 | async-start | bytes 2228224 | tf_op jit(solution)/shard_map/all_gather | solution.py:83
  8.0 279.4 %reduce-scatter.2.cloned.1.call-start = ((), (), s32[]{:S(2)}) async-start(), calls=%async_computation.3 | async-start | bytes 1572864 | tf_op jit(solution)/shard_map/reduce_scatter | solution.py:112
Sparse Core Ops, SparseCore 0:
  9.5 41.1 all-gather.3
  52.9 40.1 all-gather.5
  258.0 29.4 reduce-scatter.1
where the time goes:
time: 297 us; the launch traced here: 294 us
  waiting for transfers between devices  91.3 us (31%)
  local copies, waits for them, and re-layouts  57.4 us (19%)
  loops' own time  54.7 us (18%)
  matrix products  34 us (11%)
  other arithmetic  26.4 us (9%)
  blocking collectives  16.9 us (6%)
  between operations  13.2 us (4%)
    another operation x1, loops' own time, shards(): lax.scan(one_shard, carry, (shaped_keys, shaped_values, shard_numbers))  53 us
    all_gather x1, waiting for transfers between devices, shards(): value_piece = lax.all_gather(values, 'ctx', axis=0, tiled=True)  38.4 us
    reduce_scatter x1, waiting for transfers between devices, shards(): lax.psum_scatter(partial_terms.astype(jnp.bfloat16), 'tp', scatter_dimens...  29.6 us
    dynamic_slice x64, local copies, waits for them, and re-layouts, shards(): lax.scan(one_shard, carry, (shaped_keys, shaped_values, shard_numbers))  27 us
    all_gather x1, waiting for transfers between devices, shards(): key_piece = lax.all_gather(keys, 'ctx', axis=0, tiled=True)  21.9 us
    gather x16, local copies, waits for them, and re-layouts, one_shard(): key_doc = jnp.take(all_docs, key_pos)  18.4 us
    all_gather x1, blocking collectives, shards(): all_docs = lax.all_gather(docs, 'ctx', axis=0, tiled=True)  16.9 us
    dot_general x26, matrix products, attend(): jnp.einsum('gkij,jgd->gkid', weights.astype(jnp.bfloat16), value_part, pr...  14.9 us
  transfers between devices with their start and end apart: 3, of which 3 were waited for; matrix products, arithmetic and copies ran while one was open for 3% of the time, Pallas kernels for 0%

commit v1 on v0

v1 whole, which is shorter than its diff:
```python
import functools
import math

import jax
import jax.numpy as jnp
from jax import lax
from jax.experimental import pallas as pl
from jax.experimental.pallas import tpu as pltpu
from jax.sharding import PartitionSpec as P

HEAD_DIM = 128
LEVEL = 4
MESH = pl.DeviceIdType.MESH


def both(*terms):
    out = terms[0]
    for term in terms[1:]:
        out = jnp.logical_and(out, term)
    return out


def kernel(
    n_ctx, n_tp, far, cw,
    q_ref, doc_ref, k_hbm, v_hbm, w_hbm, out_ref,
    kv, docs, w_vmem, attn, outgoing, incoming, bias,
    stage_sem, w_sem, recv_sem, up_sem, x_sem, core_sem, hop_sem,
    doc_send, doc_recv, tp_send, tp_recv,
):
    rows = q_ref.shape[0]
    kv_heads = k_hbm.shape[1] // HEAD_DIM
    group = q_ref.shape[1] // k_hbm.shape[1]
    levels = n_ctx // LEVEL
    top = (far + LEVEL - 1) // LEVEL
    count = far + 1
    cols = out_ref.shape[1]
    chunks = cols // cw

    me = lax.axis_index("ctx")
    t = lax.axis_index("tp")
    z, r = me // LEVEL, me % LEVEL
    r1 = r + 1 - 2 * (r % 2)
    r2 = (r + 2) % LEVEL
    r3 = LEVEL - 1 - r
    base = me - r

    def needs(k, reader, owner):
        gap = LEVEL * k + reader - owner
        return both(z >= k, gap >= 0, gap <= far)

    def either(a, b):
        return jnp.logical_or(a, b)

    own = LEVEL - 1 - r
    staged = []
    for h in range(kv_heads):
        span = slice(h * HEAD_DIM, (h + 1) * HEAD_DIM)
        for i, src in enumerate((k_hbm, v_hbm)):
            c = pltpu.make_async_copy(src.at[:, span], kv.at[own, h, i], stage_sem.at[h, i])
            c.start()
            staged.append(c)

    barrier = pltpu.get_barrier_semaphore()

    def greet(device):
        pl.semaphore_signal(barrier, inc=1, device_id=device, device_id_type=MESH)

    for d in range(1, far + 1):
        @pl.when(me - d >= 0)
        def _():
            greet({"ctx": me - d})
    for other in (r1, r2):
        @pl.when(other > r)
        def _():
            greet({"ctx": base + other})
    for dt in range(1, n_tp):
        greet({"tp": (t + dt) % n_tp})
    waits = jnp.minimum(far, n_ctx - 1 - me) + (n_tp - 1)
    waits = waits + jnp.where(r1 < r, 1, 0) + jnp.where(r2 < r, 1, 0)
    pl.semaphore_wait(barrier, waits)

    docs[0] = doc_ref[...]

    def doc_copy(d):
        return pltpu.make_async_remote_copy(
            src_ref=doc_ref, dst_ref=docs.at[d], send_sem=doc_send.at[d], recv_sem=doc_recv.at[d],
            device_id={"ctx": me + d}, device_id_type=MESH)

    for d in range(1, far + 1):
        @pl.when(me + d < n_ctx)
        def _():
            doc_copy(d).start()

    def copy(src_slot, dst_slot, h, send, device):
        return pltpu.make_async_remote_copy(
            src_ref=kv.at[src_slot, h], dst_ref=kv.at[dst_slot, h],
            send_sem=send, recv_sem=recv_sem.at[dst_slot, h],
            device_id={"ctx": device}, device_id_type=MESH)

    def slot(k, owner):
        return LEVEL * k + LEVEL - 1 - owner

    def up(k, h):
        return copy(slot(k, r), slot(k + 1, r), h, up_sem.at[k, h], me + LEVEL)

    def across(k, h):
        return copy(slot(k, r), slot(k, r), h, x_sem.at[k, h], base + r2)

    def core(k, h):
        return copy(slot(k, r), slot(k, r), h, core_sem.at[k, h], base + r1)

    def hop(k, h):
        return copy(slot(k, r2), slot(k, r2), h, hop_sem.at[k, h], base + r1)

    def goes_up(k):
        return both(z >= k, z + 1 < levels, LEVEL * (k + 1) - r <= far)

    def goes_across(k):
        return either(needs(k, r2, r), needs(k, r3, r))

    def arrived(where, h):
        pltpu.make_async_copy(kv.at[where, h], kv.at[where, h], recv_sem.at[where, h]).wait()

    def column(k, h):
        if k > 0:
            @pl.when(both(z >= k, LEVEL * k - r <= far))
            def _():
                arrived(slot(k, r), h)

        @pl.when(goes_up(k))
        def _():
            up(k, h).start()

        @pl.when(goes_across(k))
        def _():
            across(k, h).start()

        @pl.when(needs(k, r1, r))
        def _():
            core(k, h).start()

    def crossed(k, h):
        @pl.when(either(needs(k, r, r2), needs(k, r1, r2)))
        def _():
            arrived(slot(k, r2), h)

        @pl.when(needs(k, r1, r2))
        def _():
            hop(k, h).start()

    def rest(k, h):
        for owner in (r1, r3):
            @pl.when(needs(k, r, owner))
            def _():
                arrived(slot(k, owner), h)

    def own_sends(h):
        staged[2 * h].wait()
        staged[2 * h + 1].wait()
        column(0, h)

    for h in range(min(2, kv_heads)):
        own_sends(h)

    w_copy = pltpu.make_async_copy(w_hbm, w_vmem, w_sem)
    w_copy.start()

    for u in range(LEVEL, kv.shape[0]):
        @pl.when(u > LEVEL * z + LEVEL - 1)
        def _():
            kv[u] = jnp.zeros(kv.shape[1:], kv.dtype)

    for d in range(1, far + 1):
        @pl.when(d > me)
        def _():
            docs[d] = jnp.full(docs.shape[1:], 1 << 30, docs.dtype)

        @pl.when(me >= d)
        def _():
            pltpu.make_async_copy(docs.at[d], docs.at[d], doc_recv.at[d]).wait()

    doc_column = jnp.transpose(jnp.broadcast_to(docs[0], (rows, rows)))
    smaller = jnp.zeros((rows, rows), jnp.int32)
    for d in range(far + 1):
        smaller = smaller + jnp.where(docs[d] < doc_column, 1, 0)
    start = jnp.sum(smaller, axis=1, keepdims=True)
    start = start + rows * jnp.maximum(me - far, 0)
    ahead = lax.broadcasted_iota(jnp.int32, (rows, rows), 1)
    position = lax.broadcasted_iota(jnp.int32, (rows, rows), 0)
    bias[0] = jnp.where((me * rows + ahead >= start) & (ahead <= position), 0.0, -1e30)
    for d in range(1, count):
        bias[d] = jnp.where((me - d) * rows + ahead >= start, 0.0, -1e30)

    scale = math.log2(math.e) / math.sqrt(HEAD_DIM)

    def attend(h, g):
        head = h * group + g
        span = slice(head * HEAD_DIM, (head + 1) * HEAD_DIM)
        query = q_ref[:, span]
        parts = []
        for d in range(count):
            s = lax.dot_general(query, kv[own + d, h, 0], (((1,), (1,)), ((), ())),
                                preferred_element_type=jnp.float32)
            parts.append(s + bias[d])
        scores = jnp.concatenate(parts, axis=1)
        peak = jnp.max(scores, axis=1, keepdims=True)
        weight = jnp.exp2((scores - peak) * scale)
        total = jnp.sum(weight, axis=1, keepdims=True)
        values = jnp.concatenate([kv[own + d, h, 1] for d in range(count)], axis=0)
        summed = jnp.dot(weight.astype(jnp.bfloat16), values, preferred_element_type=jnp.float32)
        attn[:, span] = (summed / total).astype(jnp.bfloat16)

    def service(h):
        steps = []
        if h + 1 < kv_heads and h > 0:
            steps.append(functools.partial(own_sends, h + 1))
        for k in range(1, top + 2):
            if k <= top:
                steps.append(functools.partial(column, k, h))
            steps.append(functools.partial(crossed, k - 1, h))
        return steps

    for h in range(kv_heads + 1):
        steps = service(h) if h < kv_heads else []
        if h == 0:
            for step in steps:
                step()
            continue
        for k in range(top + 1):
            rest(k, h - 1)
        per = -(-len(steps) // group)
        for g in range(group):
            attend(h - 1, g)
            for step in steps[g * per:(g + 1) * per]:
                step()

    w_copy.wait()

    def tp_copy(dt, c):
        return pltpu.make_async_remote_copy(
            src_ref=outgoing.at[dt - 1, c], dst_ref=incoming.at[dt - 1, c],
            send_sem=tp_send.at[dt - 1, c], recv_sem=tp_recv.at[dt - 1, c],
            device_id={"tp": (t + dt) % n_tp}, device_id_type=MESH)

    def project(owner, c):
        at = pl.multiple_of(owner * cols + c * cw, cw)
        return jnp.dot(attn[...], w_vmem[:, pl.ds(at, cw)], preferred_element_type=jnp.float32)

    for dt in range(1, n_tp):
        @pl.loop(0, chunks)
        def _(c):
            outgoing[dt - 1, c] = project((t + dt) % n_tp, c).astype(jnp.bfloat16)
            tp_copy(dt, c).start()

    @pl.loop(0, chunks)
    def _(c):
        total = project(t, c)
        for dt in range(1, n_tp):
            tp_copy(dt, c).wait_recv()
            total = total + incoming[dt - 1, c].astype(jnp.float32)
        out_ref[:, pl.ds(pl.multiple_of(c * cw, cw), cw)] = total.astype(out_ref.dtype)

    for dt in range(1, n_tp):
        @pl.loop(0, chunks)
        def _(c):
            tp_copy(dt, c).wait_send()
    for d in range(1, far + 1):
        @pl.when(me + d < n_ctx)
        def _():
            doc_copy(d).wait_send()
    for k in range(top + 1):
        for cond, make in ((goes_up(k), up), (goes_across(k), across),
                           (needs(k, r1, r), core), (needs(k, r1, r2), hop)):
            @pl.when(cond)
            def _():
                for h in range(kv_heads):
                    make(k, h).wait_send()


def shards(n_ctx, n_tp, queries, keys, values, docs, out_weight):
    rows = queries.shape[0]
    tokens = rows * n_ctx
    longest = tokens // 2 + rows
    far = min(n_ctx - 1, (longest - 1 + rows - 1) // rows)
    kv_heads = keys.shape[1] // HEAD_DIM
    top = (far + LEVEL - 1) // LEVEL
    slots = far + LEVEL
    cols = out_weight.shape[1] // n_tp
    cw = min(256, cols)
    chunks = cols // cw
    dma = pltpu.SemaphoreType.DMA
    anywhere = pl.BlockSpec(memory_space=pl.ANY)
    vmem = pl.BlockSpec(memory_space=pltpu.VMEM)
    return pl.pallas_call(
        functools.partial(kernel, n_ctx, n_tp, far, cw),
        out_shape=jax.ShapeDtypeStruct((rows, cols), jnp.bfloat16),
        in_specs=[vmem, vmem, anywhere, anywhere, anywhere],
        out_specs=vmem,
        scratch_shapes=[
            pltpu.VMEM((slots, kv_heads, 2, rows, HEAD_DIM), jnp.bfloat16),
            pltpu.VMEM((far + 1, 1, rows), jnp.int32),
            pltpu.VMEM(out_weight.shape, jnp.bfloat16),
            pltpu.VMEM(queries.shape, jnp.bfloat16),
            pltpu.VMEM((n_tp - 1, chunks, rows, cw), jnp.bfloat16),
            pltpu.VMEM((n_tp - 1, chunks, rows, cw), jnp.bfloat16),
            pltpu.VMEM((far + 1, rows, rows), jnp.float32),
            dma((kv_heads, 2)),
            dma,
            dma((slots, kv_heads)),
            dma((top + 1, kv_heads)),
            dma((top + 1, kv_heads)),
            dma((top + 1, kv_heads)),
            dma((top + 1, kv_heads)),
            dma((far + 1,)),
            dma((far + 1,)),
            dma((n_tp - 1, chunks)),
            dma((n_tp - 1, chunks)),
        ],
        compiler_params=pltpu.CompilerParams(
            collective_id=0, has_side_effects=True, vmem_limit_bytes=56 * 1024 * 1024
        ),
    )(queries, docs.reshape(1, rows), keys, values, out_weight)


def solution(mesh):
    placed = (P("ctx", "tp"), P("ctx", "tp"), P("ctx", "tp"), P("ctx"), P("tp", None))
    return jax.shard_map(
        functools.partial(shards, mesh.shape["ctx"], mesh.shape["tp"]),
        mesh=mesh, in_specs=placed, out_specs=P("ctx", "tp"), check_vma=False,
    )
```

time: 297 us -> 60.4 us (0.20)
  waiting for transfers between devices: 91.3 us -> 0 us
  Pallas kernels: 0 us -> 58.4 us
  local copies, waits for them, and re-layouts: 57.4 us -> 1.88 us
  loops' own time: 54.7 us -> 0 us
  matrix products: 34 us -> 0 us
  other arithmetic: 26.4 us -> 0 us
  blocking collectives: 16.9 us -> 0 us
  between operations: 13.2 us -> 0.01 us
    all_gather x2 -> x0, waiting for transfers between devices: 60.3 us -> none  [the longest x1 38.4 us: shards(): value_piece = lax.all_gather(values, 'ctx', axis=0, tiled=True)]
    pallas_call x0 -> x1, Pallas kernels: none -> 58.4 us  [shards(): pl.pallas_call(functools.partial(kernel, n_ctx, n_tp, far, cw), out_shape...]
    another operation x33 -> x0, loops' own time: 54.7 us -> none  [the longest x1 53 us: shards(): lax.scan(one_shard, carry, (shaped_keys, shaped_values, shard_numbers))]
    dot_general x53 -> x0, matrix products: 34 us -> none  [the longest x26 14.9 us: attend(): jnp.einsum('gkij,jgd->gkid', weights.astype(jnp.bfloat16), value_part, pr...]
    reduce_scatter x1 -> x0, waiting for transfers between devices: 29.6 us -> none  [shards(): lax.psum_scatter(partial_terms.astype(jnp.bfloat16), 'tp', scatter_dimens...]
    dynamic_slice x64 -> x0, local copies, waits for them, and re-layouts: 27 us -> none  [shards(): lax.scan(one_shard, carry, (shaped_keys, shaped_values, shard_numbers))]
    gather x18 -> x0, local copies, waits for them, and re-layouts: 19.9 us -> none  [the longest x16 18.4 us: one_shard(): key_doc = jnp.take(all_docs, key_pos)]
    all_gather x1 -> x0, blocking collectives: 16.9 us -> none  [shards(): all_docs = lax.all_gather(docs, 'ctx', axis=0, tiled=True)]
  transfers between devices with their start and end apart: 3 -> 0, of which waited for: 3 -> 0; matrix products, arithmetic and copies ran while one was open for 3% -> 0% of each run, Pallas kernels for 0% -> 0%
where the time goes in v1:
time: 60.4 us; the launch traced here: 60.2 us
  Pallas kernels  58.4 us (97%)
  local copies, waits for them, and re-layouts  1.88 us (3%)
    pallas_call x1, Pallas kernels, shards(): pl.pallas_call(functools.partial(kernel, n_ctx, n_tp, far, cw), out_shape...  58.4 us
    unnamed x1, local copies, waits for them, and re-layouts  1.88 us

profile of v1, /device:TPU:24, one launch (start us, length us, event | category | flops | bytes accessed | tf_op | source)
XLA Modules:
  0.0 60.2 jit_solution(1581710902367930785)
XLA Ops:
  0.0 58.4 %shard_map.55 = bf16[128,2048]{1,0:T(8,128)(2,1)} custom-call(bf16[128,2048]{1,0:T(8,128)(2,1)} %q_ref.1, s32[1,128]{1,0:T(1,128)} %bitcast.1, bf16[128,512]{1,0:T(8,128)(2,1)} %k_hbm.1, bf16[128,512]{1,0:T(8,128)(2,1)} %v_hbm.1, bf16[2048,4096]{1,0:T(8,128)(2,1)} %w_hbm.1), custom_call_target="tpu_custom_call" | custom-call | tf_op jit(solution)/shard_map/pallas_call | solution.py:294
  58.4 1.9 %copy.7 = bf16[128,2048]{1,0:T(8,128)(2,1)} copy(bf16[128,2048]{1,0:T(8,128)(2,1)} %shard_map.55) | data formatting | bytes 1048576

commit v2 on v1

--- a/solution.py
+++ b/solution.py
@@ -22,14 +22,14 @@
 
 def kernel(
     n_ctx, n_tp, far, cw,
-    q_ref, doc_ref, k_hbm, v_hbm, w_hbm, out_ref,
-    kv, docs, w_vmem, attn, outgoing, incoming, bias,
-    stage_sem, w_sem, recv_sem, up_sem, x_sem, core_sem, hop_sem,
+    q_hbm, doc_ref, k_hbm, v_hbm, w_hbm, out_ref,
+    kv, docs, q_ref, w_vmem, attn, outgoing, incoming, bias, held, peaks,
+    stage_sem, q_sem, w_sem, recv_sem, up_sem, x_sem, core_sem, hop_sem,
     doc_send, doc_recv, tp_send, tp_recv,
 ):
-    rows = q_ref.shape[0]
+    rows = q_hbm.shape[0]
     kv_heads = k_hbm.shape[1] // HEAD_DIM
-    group = q_ref.shape[1] // k_hbm.shape[1]
+    group = q_hbm.shape[1] // k_hbm.shape[1]
     levels = n_ctx // LEVEL
     top = (far + LEVEL - 1) // LEVEL
     count = far + 1
@@ -59,6 +59,8 @@
             c = pltpu.make_async_copy(src.at[:, span], kv.at[own, h, i], stage_sem.at[h, i])
             c.start()
             staged.append(c)
+    q_copy = pltpu.make_async_copy(q_hbm, q_ref, q_sem)
+    q_copy.start()
 
     barrier = pltpu.get_barrier_semaphore()
 
@@ -148,19 +150,17 @@
         def _():
             hop(k, h).start()
 
-    def rest(k, h):
-        for owner in (r1, r3):
-            @pl.when(needs(k, r, owner))
-            def _():
-                arrived(slot(k, owner), h)
-
-    def own_sends(h):
+    def rest(first, last, h):
+        for k in range(first, last + 1):
+            for owner in (r1, r3):
+                @pl.when(needs(k, r, owner))
+                def _():
+                    arrived(slot(k, owner), h)
+
+    for h in range(kv_heads):
         staged[2 * h].wait()
         staged[2 * h + 1].wait()
         column(0, h)
-
-    for h in range(min(2, kv_heads)):
-        own_sends(h)
 
     w_copy = pltpu.make_async_copy(w_hbm, w_vmem, w_sem)
     w_copy.start()
@@ -187,52 +187,60 @@
     start = start + rows * jnp.maximum(me - far, 0)
     ahead = lax.broadcasted_iota(jnp.int32, (rows, rows), 1)
     position = lax.broadcasted_iota(jnp.int32, (rows, rows), 0)
-    bias[0] = jnp.where((me * rows + ahead >= start) & (ahead <= position), 0.0, -1e30)
+    bias[:, :rows] = jnp.where((me * rows + ahead >= start) & (ahead <= position), 0.0, -1e30)
     for d in range(1, count):
-        bias[d] = jnp.where((me - d) * rows + ahead >= start, 0.0, -1e30)
+        bias[:, d * rows:(d + 1) * rows] = jnp.where((me - d) * rows + ahead >= start, 0.0, -1e30)
 
     scale = math.log2(math.e) / math.sqrt(HEAD_DIM)
 
-    def attend(h, g):
-        head = h * group + g
-        span = slice(head * HEAD_DIM, (head + 1) * HEAD_DIM)
-        query = q_ref[:, span]
-        parts = []
-        for d in range(count):
-            s = lax.dot_general(query, kv[own + d, h, 0], (((1,), (1,)), ((), ())),
-                                preferred_element_type=jnp.float32)
-            parts.append(s + bias[d])
-        scores = jnp.concatenate(parts, axis=1)
+    def attend(h, first, blocks, begin, end):
+        heads = range(h * group + first, h * group + first + batch)
+        wide = batch * rows
+        at = pl.ds(first * rows, wide)
+        query = jnp.concatenate(
+            [q_ref[:, e * HEAD_DIM:(e + 1) * HEAD_DIM] for e in heads], axis=0)
+        keys = jnp.concatenate([kv[own + d, h, 0] for d in blocks], axis=0)
+        values = jnp.concatenate([kv[own + d, h, 1] for d in blocks], axis=0)
+        values = jnp.concatenate([values, jnp.ones_like(values)], axis=1)
+        scores = lax.dot_general(query, keys, (((1,), (1,)), ((), ())),
+                                 preferred_element_type=jnp.float32)
+        mask = bias[:, blocks[0] * rows:(blocks[-1] + 1) * rows]
+        scores = (scores.reshape(batch, rows, -1) + mask[None]).reshape(wide, -1)
         peak = jnp.max(scores, axis=1, keepdims=True)
-        weight = jnp.exp2((scores - peak) * scale)
-        total = jnp.sum(weight, axis=1, keepdims=True)
-        values = jnp.concatenate([kv[own + d, h, 1] for d in range(count)], axis=0)
-        summed = jnp.dot(weight.astype(jnp.bfloat16), values, preferred_element_type=jnp.float32)
-        attn[:, span] = (summed / total).astype(jnp.bfloat16)
-
-    def service(h):
-        steps = []
-        if h + 1 < kv_heads and h > 0:
-            steps.append(functools.partial(own_sends, h + 1))
-        for k in range(1, top + 2):
-            if k <= top:
-                steps.append(functools.partial(column, k, h))
-            steps.append(functools.partial(crossed, k - 1, h))
-        return steps
-
-    for h in range(kv_heads + 1):
-        steps = service(h) if h < kv_heads else []
-        if h == 0:
-            for step in steps:
-                step()
-            continue
-        for k in range(top + 1):
-            rest(k, h - 1)
-        per = -(-len(steps) // group)
-        for g in range(group):
-            attend(h - 1, g)
-            for step in steps[g * per:(g + 1) * per]:
-                step()
+        if not begin:
+            earlier = peaks[h, at]
+            peak = jnp.maximum(peak, earlier)
+            rescale = jnp.exp2((earlier - peak) * scale)
+        weight = jnp.exp2((scores - peak) * scale).astype(jnp.bfloat16)
+        summed = jnp.dot(weight, values, preferred_element_type=jnp.float32)
+        if not begin:
+            summed = summed + held[h, at] * rescale
+        if end:
+            result = summed[:, :HEAD_DIM] / summed[:, HEAD_DIM:]
+            for i, e in enumerate(heads):
+                attn[:, e * HEAD_DIM:(e + 1) * HEAD_DIM] = (
+                    result[i * rows:(i + 1) * rows].astype(jnp.bfloat16))
+        else:
+            peaks[h, at] = peak
+            held[h, at] = summed
+
+    near = top // 2
+    split = LEVEL * near + 1
+    batch = 2
+    q_copy.wait()
+    for k in range(1, top + 1):
+        for h in range(kv_heads):
+            column(k, h)
+            crossed(k - 1, h)
+            if k == near + 1:
+                rest(0, near, h)
+                for g in range(0, group, batch):
+                    attend(h, g, range(split), True, split == count)
+            if k == top:
+                crossed(k, h)
+                rest(near + 1, top, h)
+                for g in range(0, group, batch):
+                    attend(h, g, range(split, count), False, True)
 
     w_copy.wait()
 
@@ -283,6 +291,7 @@
     longest = tokens // 2 + rows
     far = min(n_ctx - 1, (longest - 1 + rows - 1) // rows)
     kv_heads = keys.shape[1] // HEAD_DIM
+    group = queries.shape[1] // keys.shape[1]
     top = (far + LEVEL - 1) // LEVEL
     slots = far + LEVEL
     cols = out_weight.shape[1] // n_tp
@@ -294,17 +303,21 @@
     return pl.pallas_call(
         functools.partial(kernel, n_ctx, n_tp, far, cw),
         out_shape=jax.ShapeDtypeStruct((rows, cols), jnp.bfloat16),
-        in_specs=[vmem, vmem, anywhere, anywhere, anywhere],
+        in_specs=[anywhere, vmem, anywhere, anywhere, anywhere],
         out_specs=vmem,
         scratch_shapes=[
             pltpu.VMEM((slots, kv_heads, 2, rows, HEAD_DIM), jnp.bfloat16),
             pltpu.VMEM((far + 1, 1, rows), jnp.int32),
+            pltpu.VMEM(queries.shape, jnp.bfloat16),
             pltpu.VMEM(out_weight.shape, jnp.bfloat16),
             pltpu.VMEM(queries.shape, jnp.bfloat16),
             pltpu.VMEM((n_tp - 1, chunks, rows, cw), jnp.bfloat16),
             pltpu.VMEM((n_tp - 1, chunks, rows, cw), jnp.bfloat16),
-            pltpu.VMEM((far + 1, rows, rows), jnp.float32),
+            pltpu.VMEM((rows, (far + 1) * rows), jnp.float32),
+            pltpu.VMEM((kv_heads, group * rows, 2 * HEAD_DIM), jnp.float32),
+            pltpu.VMEM((kv_heads, group * rows, 1), jnp.float32),
             dma((kv_heads, 2)),
+            dma,
             dma,
             dma((slots, kv_heads)),
             dma((top + 1, kv_heads)),

time: 60.4 us -> 47.8 us (0.79)
  Pallas kernels: 58.4 us -> 45.4 us
    pallas_call x1, Pallas kernels: 58.4 us -> 45.4 us  [shards(): pl.pallas_call(functools.partial(kernel, n_ctx, n_tp, far, cw), out_shape...]
where the time goes in v2:
time: 47.8 us; the launch traced here: 47.3 us
  Pallas kernels  45.4 us (95%)
  local copies, waits for them, and re-layouts  1.88 us (4%)
    pallas_call x1, Pallas kernels, shards(): pl.pallas_call(functools.partial(kernel, n_ctx, n_tp, far, cw), out_shape...  45.4 us
    unnamed x1, local copies, waits for them, and re-layouts  1.88 us

profile of v2, /device:TPU:24, one launch (start us, length us, event | category | flops | bytes accessed | tf_op | source)
XLA Modules:
  0.0 47.3 jit_solution(1440661204455402182)
XLA Ops:
  0.0 45.4 %shard_map.55 = bf16[128,2048]{1,0:T(8,128)(2,1)} custom-call(bf16[128,2048]{1,0:T(8,128)(2,1)} %q_hbm.1, s32[1,128]{1,0:T(1,128)} %bitcast.1, bf16[128,512]{1,0:T(8,128)(2,1)} %k_hbm.1, bf16[128,512]{1,0:T(8,128)(2,1)} %v_hbm.1, bf16[2048,4096]{1,0:T(8,128)(2,1)} %w_hbm.1), custom_call_target="tpu_custom_call" | custom-call | tf_op jit(solution)/shard_map/pallas_call | solution.py:303
  45.4 1.9 %copy.7 = bf16[128,2048]{1,0:T(8,128)(2,1)} copy(bf16[128,2048]{1,0:T(8,128)(2,1)} %shard_map.55) | data formatting | bytes 1048576
